TPU v7x, 32 devices: a whole 2x2x4 slice. The times are simulated.
32 devices in a mesh: sector: 8 (over z, y), mpo: 4 (over x, core).
Axes of the slice: x: 2, y: 2, z: 4, core: 2. Of those that a mesh axis runs over, the one named last changes fastest.
Arguments:
- guess: float32 [128, 128, 128], P('sector'), may hold values from -64 to 64
- diag_shift: float32 [128, 128, 128], P('sector'), may hold values from 0 to 6
- block_rows: int32 [128], P('sector'), may hold values from 64 to 128
- block_cols: int32 [128], P('sector'), may hold values from 64 to 128
- left_env: bfloat16 [64, 128, 128, 128], P('mpo', 'sector'), may hold values from -2 to 2
- right_env: bfloat16 [64, 128, 128, 128], P('mpo', 'sector'), may hold values from -2 to 2
- edge_input: int32 [256], P('sector'), may hold values from 0 to 15
- edge_left: int32 [256], P('sector'), may hold values from 0 to 15
- edge_right: int32 [256], P('sector'), may hold values from 0 to 15
- edge_owner: int32 [256, 1], P('sector'), may hold values from 0 to 7, as said below
- edge_slot: int32 [256], P('sector'), may hold values from 0 to 15, as said below
Outputs:
- images: float32 [3, 128, 128, 128], P(None, 'sector', 'mpo')
- next_basis: float32 [128, 128, 128], P('sector', 'mpo')
- ritz: float32 [3], replicated
Inputs may be any that keep to these rules, and one draw needn't show every extreme that they name: `edge_owner`: among the 32 couplings of one index of sector, at most 8 name the same owner, and some owner is named by exactly 8. No coupling names the index of sector that holds it. `edge_slot`: couplings come in mirrored pairs: for every coupling e there is a coupling f with in_f = out_e and out_f = in_e.
All inputs are finite; a program needn't handle non-finite values.
Results may differ from a plain program's by a relative error of at most 0.025.
Values may be sent and summed in bfloat16 or wider, within the bound.
A program may use at most 64 MiB of HBM per device.

v0:
```python
import jax
import jax.numpy as jnp
from jax import lax
from jax.sharding import PartitionSpec as P

APPLIES = 3


def per_device(
    guess,
    diag_shift,
    block_rows,
    block_cols,
    left_env,
    right_env,
    edge_input,
    edge_left,
    edge_right,
    edge_owner,
    edge_slot,
):
    slots, size, _ = guess.shape
    sectors = lax.axis_size("sector")
    terms_count = lax.axis_size("mpo")
    edges = edge_input.shape[0]
    capacity = max(2, 2 * edges // sectors)
    share = size // terms_count
    first_row = lax.axis_index("mpo") * share
    owner = edge_owner[:, 0]
    order = jnp.arange(edges, dtype=jnp.int32)
    earlier = (owner[:, None] == owner[None, :]) & (order[None, :] < order[:, None])
    rank = jnp.sum(earlier.astype(jnp.int32), axis=1)
    where_to = owner * capacity + rank
    place_hits = where_to[None, :] == jnp.arange(sectors * capacity, dtype=jnp.int32)[:, None]
    placing = place_hits.astype(jnp.bfloat16)
    slot_ids = (jnp.sum(jnp.where(place_hits, edge_slot[None, :] + 1, 0), axis=1) - 1).reshape(
        sectors, capacity
    )
    rows_index = lax.broadcasted_iota(jnp.int32, guess.shape, 1)
    cols_index = lax.broadcasted_iota(jnp.int32, guess.shape, 2)
    mask = (
        (rows_index < block_rows[:, None, None]) & (cols_index < block_cols[:, None, None])
    ).astype(jnp.float32)

    def own_rows(values, axis):
        return lax.dynamic_slice_in_dim(values, first_row, share, axis)

    def add_up(values):
        return lax.psum(values, "sector")

    def to_input(vector):
        return vector.astype(jnp.bfloat16)

    def deliver(total):
        rounded = total.astype(jnp.bfloat16)
        whole = lax.all_gather(rounded, "mpo", axis=1, tiled=True)
        packed = jnp.dot(
            placing, whole.reshape(edges, size * size), preferred_element_type=jnp.float32
        )
        packed = packed.astype(jnp.bfloat16).reshape(sectors, capacity, size, size)
        return (
            lax.all_to_all(packed, "sector", split_axis=0, concat_axis=0, tiled=True),
            lax.all_to_all(slot_ids, "sector", split_axis=0, concat_axis=0, tiled=True),
        )

    def apply_hamiltonian(vector):
        xin = to_input(vector)
        picked = xin[edge_input]

        def one_term(total, envs):
            left_term, right_term = envs
            half = jnp.einsum(
                "eij,ejk->eik", picked, right_term[edge_right], preferred_element_type=jnp.float32
            )
            half = half.astype(jnp.bfloat16)
            return (
                total
                + jnp.einsum(
                    "eij,ejk->eik", left_term[edge_left], half, preferred_element_type=jnp.float32
                ),
                None,
            )

        partial_sum, _ = lax.scan(
            one_term, jnp.zeros((edges, size, size), jnp.float32), (left_env, right_env)
        )
        rounded_terms = partial_sum.astype(jnp.bfloat16).astype(jnp.float32)
        total = lax.psum_scatter(
            rounded_terms.astype(jnp.bfloat16), "mpo", scatter_dimension=1, tiled=True
        ).astype(jnp.float32)
        arrived, arrived_ids = deliver(total)
        taking = (
            arrived_ids.reshape(-1)[None, :] == jnp.arange(slots, dtype=jnp.int32)[:, None]
        ).astype(jnp.bfloat16)
        gathered = jnp.dot(
            taking, arrived.reshape(sectors * capacity, -1), preferred_element_type=jnp.float32
        )
        return gathered.reshape(mask.shape) * mask

    start = mask * guess
    basis = [start / jnp.sqrt(add_up(jnp.sum(start * start)) + 1e-06)]
    image_list = []
    ritz_list = []
    for step in range(APPLIES):
        current = basis[-1]
        image = apply_hamiltonian(current)
        image_list.append(image)
        theta = add_up(jnp.sum(current * image))
        ritz_list.append(theta)
        corr = mask * (image - theta * current) / jnp.maximum(jnp.abs(diag_shift - theta), 1.0)
        sums = add_up(tuple((jnp.sum(vector * corr) for vector in basis)) + (jnp.sum(corr * corr),))
        projections = sums[:-1]
        ortho = corr
        length = sums[-1]
        for weight, vector in zip(projections, basis):
            ortho = ortho - weight * vector
            length = length - weight * weight
        basis.append(ortho / jnp.sqrt(length + 1e-06))
    stacked = jnp.stack(image_list)
    final = basis[-1]
    stacked = own_rows(stacked, 2)
    final = own_rows(final, 1)
    return (stacked, final, jnp.stack(ritz_list))


def solution(mesh):
    return jax.shard_map(
        per_device,
        mesh=mesh,
        in_specs=(
            P("sector", None, None),
            P("sector", None, None),
            P("sector"),
            P("sector"),
            P("mpo", "sector", None, None),
            P("mpo", "sector", None, None),
            P("sector"),
            P("sector"),
            P("sector"),
            P("sector", None),
            P("sector"),
        ),
        out_specs=(P(None, "sector", "mpo", None), P("sector", "mpo", None), P()),
        check_vma=False,
    )
```

profile of v0, /device:TPU:0, one launch (start us, length us, event | category | flops | bytes accessed | tf_op | source)
XLA Modules:
  0.0 886.5 jit_solution(8665236364293420449)
XLA Ops:
  9.8 23.7 %psum.91 = f32[]{:T(128)} all-reduce(f32[]{:T(128)} %multiply_reduce_fusion.12), channel_id=1, replica_groups=mesh['sector'=8,'mpo'=4] {'sector'}, use_global_device_ids=true, to_apply=%region_3.4 | all-reduce | flops 1 | bytes 8 | tf_op jit(solution)/shard_map/psum | solution.py:49
  39.0 122.8 %while.33 = (s32[]{:T(128)}, f32[32,128,128]{2,1,0:T(8,128)}, bf16[16,16,128,128]{3,2,1,0:T(8,128)(2,1)}, s32[32]{0:T(128)S(1)}, bf16[16,16,128,128]{3,2,1,0:T(8...) while((s32[]{:T(128)}, f32[32,128,128]{2,1,0:T(8,128)}, ...), condition=%wide.region_5.6_spmd.clone, body=%wide.region_4.5_spmd.clone.sunk | while | flops 270010560 | bytes 13640811 | solution.py:84
  56.6 4.9 select_add_fusion.6
  164.7 22.3 %reduce-scatter.4.cloned.1.call-done = bf16[32,32,128]{2,1,0:T(8,128)(2,1)} async-done(((bf16[32,128,128]{2,1,0:T(8,128)(2,1)}), bf16[32,32,128]{2,1,0:T(8,128)(2,1)}) %reduce-scatter.4.cloned.1.call-update) | async-done | bytes 262160 | tf_op jit(solution)/shard_map/reduce_scatter | solution.py:88
  188.0 5.5 all-to-all-start
  193.5 11.9 %all-gather.4.cloned.1.call-done = bf16[32,128,128]{2,1,0:T(8,128)(2,1)} async-done(((bf16[32,32,128]{2,1,0:T(8,128)(2,1)}), bf16[32,128,128]{2,1,0:T(8,128)(2,1)}) %all-gather.4.cloned.1.call-update) | async-done | bytes 1048592 | tf_op jit(solution)/shard_map/all_gather | solution.py:56
  208.8 5.7 all-to-all-start.1
  215.8 47.3 %all-to-all-done.1 = bf16[8,8,128,128]{3,1,2,0:T(8,128)(2,1)S(1)} async-done(((bf16[8,8,128,128]{3,1,2,0:T(8,128)(2,1)}), bf16[8,8,128,128]{3,1,2,0:T(8,128)(2,1)S(1)}, u32[]{:S(2)}, u32[]{:S(2)}) %all-to-all-start.1) | async-done | bytes 2097184 | tf_op jit(solution)/shard_map/all_to_all | solution.py:62
  267.1 20.1 %psum.92 = f32[]{:T(128)} all-reduce(f32[]{:T(128)} %get-tuple-element.306), channel_id=1, replica_groups=mesh['sector'=8,'mpo'=4] {'sector'}, use_global_device_ids=true, to_apply=%region_8.9 | all-reduce | flops 1 | bytes 8 | tf_op jit(solution)/shard_map/psum | solution.py:49
  290.3 17.8 %all-reduce.2 = (f32[]{:T(128)}, f32[]{:T(128)}) all-reduce(f32[]{:T(128)} %get-tuple-element.233, f32[]{:T(128)} %get-tuple-element.232), channel_id=1, replica_groups=mesh['sector'=8,'mpo'=4] {'sector'}, use_global_device_ids=true, to_apply=%region_12.13 | all-reduce | flops 2 | bytes 16 | tf_op jit(solution)/shard_map/psum | solution.py:49
  314.9 122.8 %while.34 = (s32[]{:T(128)}, f32[32,128,128]{2,1,0:T(8,128)}, bf16[16,16,128,128]{3,2,1,0:T(8,128)(2,1)}, s32[32]{0:T(128)S(1)}, bf16[16,16,128,128]{3,2,1,0:T(8...) while((s32[]{:T(128)}, f32[32,128,128]{2,1,0:T(8,128)}, ...), condition=%wide.region_14.15_spmd.clone, body=%wide.region_13.14_spmd.clone.sunk | while | flops 270010560 | bytes 13640811 | solution.py:84
  440.6 22.7 %reduce-scatter.6.cloned.1.call-done = bf16[32,32,128]{2,1,0:T(8,128)(2,1)} async-done(((bf16[32,128,128]{2,1,0:T(8,128)(2,1)}), bf16[32,32,128]{2,1,0:T(8,128)(2,1)}) %reduce-scatter.6.cloned.1.call-update) | async-done | bytes 262160 | tf_op jit(solution)/shard_map/reduce_scatter | solution.py:88
  463.3 18.2 %all-gather.6.cloned.1.call-done = bf16[32,128,128]{2,1,0:T(8,128)(2,1)} async-done(((bf16[32,32,128]{2,1,0:T(8,128)(2,1)}), bf16[32,128,128]{2,1,0:T(8,128)(2,1)}) %all-gather.6.cloned.1.call-update) | async-done | bytes 1048592 | tf_op jit(solution)/shard_map/all_gather | solution.py:56
  485.0 5.6 all-to-all-start.2
  490.7 48.7 %all-to-all-done.2 = bf16[8,8,128,128]{3,1,2,0:T(8,128)(2,1)} async-done(((bf16[8,8,128,128]{3,1,2,0:T(8,128)(2,1)}), bf16[8,8,128,128]{3,1,2,0:T(8,128)(2,1)}, u32[]{:S(2)}, u32[]{:S(2)}) %all-to-all-start.2) | async-done | bytes 2097184 | tf_op jit(solution)/shard_map/all_to_all | solution.py:62
  543.1 20.3 %psum.95 = f32[]{:T(128)} all-reduce(f32[]{:T(128)} %get-tuple-element.308), channel_id=1, replica_groups=mesh['sector'=8,'mpo'=4] {'sector'}, use_global_device_ids=true, to_apply=%region_17.18 | all-reduce | flops 1 | bytes 8 | tf_op jit(solution)/shard_map/psum | solution.py:49
  567.6 17.8 %all-reduce.1 = (f32[]{:T(128)}, f32[]{:T(128)}, f32[]{:T(128)}) all-reduce(f32[]{:T(128)} %get-tuple-element.230, f32[]{:T(128)} %get-tuple-element.231, f32[]{:T(128)} %get-tuple-element.229), channel_id=1, replica_groups=mesh['sector'=8,'mpo'=4] {'sector'}, use_global_device_ids=true, to_apply=%region_23.24 | all-reduce | flops 3 | bytes 24 | tf_op jit(solution)/shard_map/psum | solution.py:49
  594.2 122.8 %while.35 = (s32[]{:T(128)}, f32[32,128,128]{2,1,0:T(8,128)}, bf16[16,16,128,128]{3,2,1,0:T(8,128)(2,1)}, s32[32]{0:T(128)S(1)}, bf16[16,16,128,128]{3,2,1,0:T(8...) while((s32[]{:T(128)}, f32[32,128,128]{2,1,0:T(8,128)}, ...), condition=%wide.region_25.26_spmd.clone, body=%wide.region_24.25_spmd.clone.sunk | while | flops 270010560 | bytes 13640811 | solution.py:84
  719.8 22.8 %reduce-scatter.8.cloned.1.call-done = bf16[32,32,128]{2,1,0:T(8,128)(2,1)} async-done(((bf16[32,128,128]{2,1,0:T(8,128)(2,1)}), bf16[32,32,128]{2,1,0:T(8,128)(2,1)}) %reduce-scatter.8.cloned.1.call-update) | async-done | bytes 262160 | tf_op jit(solution)/shard_map/reduce_scatter | solution.py:88
  742.6 18.2 %all-gather.8.cloned.1.call-done = bf16[32,128,128]{2,1,0:T(8,128)(2,1)} async-done(((bf16[32,32,128]{2,1,0:T(8,128)(2,1)}), bf16[32,128,128]{2,1,0:T(8,128)(2,1)}) %all-gather.8.cloned.1.call-update) | async-done | bytes 1048592 | tf_op jit(solution)/shard_map/all_gather | solution.py:56
  764.3 5.6 all-to-all-start.3
  770.0 48.6 %all-to-all-done.3 = bf16[8,8,128,128]{3,1,2,0:T(8,128)(2,1)S(1)} async-done(((bf16[8,8,128,128]{3,1,2,0:T(8,128)(2,1)}), bf16[8,8,128,128]{3,1,2,0:T(8,128)(2,1)S(1)}, u32[]{:S(2)}, u32[]{:S(2)}) %all-to-all-start.3) | async-done | bytes 2097184 | tf_op jit(solution)/shard_map/all_to_all | solution.py:62
  823.7 20.2 %psum.99 = f32[]{:T(128)} all-reduce(f32[]{:T(128)} %get-tuple-element.310), channel_id=1, replica_groups=mesh['sector'=8,'mpo'=4] {'sector'}, use_global_device_ids=true, to_apply=%region_28.29 | all-reduce | flops 1 | bytes 8 | tf_op jit(solution)/shard_map/psum | solution.py:49
  848.7 17.8 %all-reduce = (f32[]{:T(128)}, f32[]{:T(128)}, f32[]{:T(128)}, f32[]{:T(128)}) all-reduce(f32[]{:T(128)} %get-tuple-element.226, f32[]{:T(128)} %get-tuple-element.228, f32[]{:T(128)} %get-tuple-element.227, f32[]{:T(128)} %get-tuple-element.225), channel_id=1, replica_groups=mesh['sector'=8,'mpo'=4] {'sector'}, use_global_device_ids=true, to_apply=%region_36.37 | all-reduce | flops 4 | bytes 32 | tf_op jit(solution)/shard_map/psum | solution.py:49
  (427 shorter events, 433.7 us)
Async XLA Ops:
  7.2 30.0 %copy-start.16 = (s32[32]{0:T(128)S(1)}, s32[32]{0:T(128)}, u32[]{:S(2)}) copy-start(s32[32]{0:T(128)} %param.23) | copy-start | bytes 388
  7.2 179.8 %reduce-scatter.4.cloned.1.call-start = ((), (), s32[]{:S(2)}) async-start(), calls=%async_computation.7 | async-start | bytes 1310720 | tf_op jit(solution)/shard_map/reduce_scatter | solution.py:88
  161.9 25.1 %copy-start.18 = (s32[32,1]{0,1:T(1,128)S(1)}, s32[32,1]{0,1:T(1,128)}, u32[]{:S(2)}) copy-start(s32[32,1]{0,1:T(1,128)} %param.26) | copy-start | bytes 388
  161.9 25.3 %copy-start.17 = (s32[32]{0:T(128)S(1)}, s32[32]{0:T(128)}, u32[]{:S(2)}) copy-start(s32[32]{0:T(128)} %param.27) | copy-start | bytes 388
  164.7 40.7 %all-gather.4.cloned.1.call-start = ((), (), s32[]{:S(2)}) async-start(), calls=%async_computation.8 | async-start | bytes 1310720 | tf_op jit(solution)/shard_map/all_gather | solution.py:56
  188.0 20.8 %all-to-all-start = ((s32[8,1,8]{2,1,0:T(1,128)}), s32[8,1,8]{2,1,0:T(1,128)S(1)}, u32[]{:S(2)}, u32[]{:S(2)}) async-start(s32[8,1,8]{2,1,0:T(1,128)} %bitcast.1), calls=%async_computation | async-start | bytes 8192 | tf_op jit(solution)/shard_map/all_to_all | solution.py:63
  208.8 55.6 %copy-start = (f32[16,128,128]{2,0,1:T(8,128)S(1)}, f32[16,128,128]{2,0,1:T(8,128)}, u32[]{:S(2)}) copy-start(f32[16,128,128]{2,0,1:T(8,128)} %get-tuple-element.293) | copy-start | bytes 3145732
  208.8 55.6 %copy-start.14 = (s32[16]{0:T(128)S(1)}, s32[16]{0:T(128)}, u32[]{:S(2)}) copy-start(s32[16]{0:T(128)} %param.20) | copy-start | bytes 196
  208.8 55.6 %copy-start.15 = (s32[16]{0:T(128)S(1)}, s32[16]{0:T(128)}, u32[]{:S(2)}) copy-start(s32[16]{0:T(128)} %param.19) | copy-start | bytes 196
  208.8 54.3 %all-to-all-start.1 = ((bf16[8,8,128,128]{3,1,2,0:T(8,128)(2,1)}), bf16[8,8,128,128]{3,1,2,0:T(8,128)(2,1)S(1)}, u32[]{:S(2)}, u32[]{:S(2)}) async-start(bf16[8,8,128,128]{3,1,2,0:T(8,128)(2,1)} %fusion.15), calls=%async_computation.2 | async-start | bytes 4194304 | tf_op jit(solution)/shard_map/all_to_all | solution.py:62
  214.4 248.9 %reduce-scatter.6.cloned.1.call-start = ((), (), s32[]{:S(2)}) async-start(), calls=%async_computation.9 | async-start | bytes 1310720 | tf_op jit(solution)/shard_map/reduce_scatter | solution.py:88
  264.4 22.9 %copy-start.6 = (f32[16,128,128]{2,1,0:T(8,128)S(1)}, f32[16,128,128]{2,1,0:T(8,128)}, u32[]{:S(2)}) copy-start(f32[16,128,128]{2,1,0:T(8,128)} %param.18) | copy-start | bytes 3145732
  267.1 23.2 %copy-start.9 = (f32[16,128,128]{2,0,1:T(8,128)}, f32[16,128,128]{2,0,1:T(8,128)S(1)}, u32[]{:S(2)}) copy-start(f32[16,128,128]{2,0,1:T(8,128)S(1)} %get-tuple-element.307) | copy-start | bytes 3145732
  440.5 41.0 %all-gather.6.cloned.1.call-start = ((), (), s32[]{:S(2)}) async-start(), calls=%async_computation.10 | async-start | bytes 1310720 | tf_op jit(solution)/shard_map/all_gather | solution.py:56
  485.0 54.4 %copy-start.3 = (f32[16,128,128]{2,0,1:T(8,128)S(1)}, f32[16,128,128]{2,0,1:T(8,128)}, u32[]{:S(2)}) copy-start(f32[16,128,128]{2,0,1:T(8,128)} %get-tuple-element.290) | copy-start | bytes 3145732
  485.0 54.4 %all-to-all-start.2 = ((bf16[8,8,128,128]{3,1,2,0:T(8,128)(2,1)}), bf16[8,8,128,128]{3,1,2,0:T(8,128)(2,1)}, u32[]{:S(2)}, u32[]{:S(2)}) async-start(bf16[8,8,128,128]{3,1,2,0:T(8,128)(2,1)} %fusion.16), calls=%async_computation.4 | async-start | bytes 4194304 | tf_op jit(solution)/shard_map/all_to_all | solution.py:62
  490.6 252.0 %reduce-scatter.8.cloned.1.call-start = ((), (), s32[]{:S(2)}) async-start(), calls=%async_computation.11 | async-start | bytes 1310720 | tf_op jit(solution)/shard_map/reduce_scatter | solution.py:88
  539.3 24.0 %copy-start.1 = (f32[16,128,128]{2,0,1:T(8,128)S(1)}, f32[16,128,128]{2,0,1:T(8,128)}, u32[]{:S(2)}) copy-start(f32[16,128,128]{2,0,1:T(8,128)} %get-tuple-element.293) | copy-start | bytes 3145732
  539.4 24.0 %copy-start.7 = (f32[16,128,128]{2,1,0:T(8,128)S(1)}, f32[16,128,128]{2,1,0:T(8,128)}, u32[]{:S(2)}) copy-start(f32[16,128,128]{2,1,0:T(8,128)} %param.18) | copy-start | bytes 3145732
  719.8 41.1 %all-gather.8.cloned.1.call-start = ((), (), s32[]{:S(2)}) async-start(), calls=%async_computation.12 | async-start | bytes 1310720 | tf_op jit(solution)/shard_map/all_gather | solution.py:56
  764.3 55.6 %copy-start.5 = (f32[16,128,128]{2,0,1:T(8,128)S(1)}, f32[16,128,128]{2,0,1:T(8,128)}, u32[]{:S(2)}) copy-start(f32[16,128,128]{2,0,1:T(8,128)} %get-tuple-element.287) | copy-start | bytes 3145732
  764.3 54.3 %all-to-all-start.3 = ((bf16[8,8,128,128]{3,1,2,0:T(8,128)(2,1)}), bf16[8,8,128,128]{3,1,2,0:T(8,128)(2,1)S(1)}, u32[]{:S(2)}, u32[]{:S(2)}) async-start(bf16[8,8,128,128]{3,1,2,0:T(8,128)(2,1)} %fusion.17), calls=%async_computation.6 | async-start | bytes 4194304 | tf_op jit(solution)/shard_map/all_to_all | solution.py:62
  820.0 23.9 %copy-start.2 = (f32[16,128,128]{2,0,1:T(8,128)S(1)}, f32[16,128,128]{2,0,1:T(8,128)}, u32[]{:S(2)}) copy-start(f32[16,128,128]{2,0,1:T(8,128)} %get-tuple-element.293) | copy-start | bytes 3145732
  820.0 23.9 %copy-start.4 = (f32[16,128,128]{2,0,1:T(8,128)S(1)}, f32[16,128,128]{2,0,1:T(8,128)}, u32[]{:S(2)}) copy-start(f32[16,128,128]{2,0,1:T(8,128)} %get-tuple-element.290) | copy-start | bytes 3145732
  (5 other events, 10.2 us)
Sparse Core Ops, SparseCore 0:
  164.8 22.1 reduce-scatter.3
  188.6 16.7 all-gather.3
  440.6 22.6 reduce-scatter.5
  464.7 16.7 all-gather.5
  719.9 22.6 reduce-scatter.7
  744.1 16.7 all-gather.7
where the time goes:
time: 890 us; the launch traced here: 886 us
  waiting for transfers between devices  261 us (29%)
  matrix products  253 us (28%)
  local copies, waits for them, and re-layouts  144 us (16%)
  blocking collectives  138 us (16%)
  other arithmetic  41.1 us (5%)
  between operations  24.8 us (3%)
  starting transfers between devices  22.7 us (3%)
    dot_general x48, matrix products, one_term(): jnp.einsum('eij,ejk->eik', left_term[edge_left], half, preferred_element_...  233 us
    all_to_all x3, waiting for transfers between devices, deliver(): lax.all_to_all(packed, 'sector', split_axis=0, concat_axis=0, tiled=True)  145 us
    psum x7, blocking collectives, add_up(): return lax.psum(values, 'sector')  138 us
    reduce_scatter x3, waiting for transfers between devices, apply_hamiltonian(): lax.psum_scatter(rounded_terms.astype(jnp.bfloat16), 'mpo', scatter_dimen...  67.8 us
    squeeze x48, local copies, waits for them, and re-layouts, apply_hamiltonian(): lax.scan(one_term, jnp.zeros((edges, size, size), jnp.float32), (left_env...  60.9 us
    all_gather x3, waiting for transfers between devices, deliver(): whole = lax.all_gather(rounded, 'mpo', axis=1, tiled=True)  48.3 us
    gather x48, local copies, waits for them, and re-layouts, one_term(): left_term[edge_left]  35.9 us
    gather x48, local copies, waits for them, and re-layouts, one_term(): right_term[edge_right]  35.9 us
  transfers between devices with their start and end apart: 10, of which 9 were waited for; matrix products, arithmetic and copies ran while one was open for 1% of the time, Pallas kernels for 0%

commit v1 on v0

v1 whole, which is shorter than its diff:
```python
import functools

import jax
import jax.numpy as jnp
from jax import lax
from jax.experimental import pallas as pl
from jax.experimental.pallas import tpu as pltpu
from jax.sharding import PartitionSpec as P

APPLIES = 3
CHUNKS = 4
GROUP = 4
MESH = pl.DeviceIdType.MESH


def davidson_kernel(
    sectors,
    ranks,
    capacity,
    in_ref,
    left_ref,
    right_ref,
    source_ref,
    perm_ref,
    keep_ref,
    last_ref,
    has_ref,
    start_ref,
    mask_ref,
    diag_ref,
    lenv_hbm,
    renv_hbm,
    images_ref,
    next_ref,
    ritz_ref,
    lenv,
    renv,
    basis,
    gathered,
    parts,
    part_in,
    total,
    packed,
    arrived,
    running,
    gram,
    sum_m,
    sum_s,
    env_sem,
    x_send,
    x_recv,
    p_send,
    p_recv,
    a_send,
    a_recv,
    sm_send,
    sm_recv,
    ss_send,
    ss_recv,
):
    terms, _, size, _ = lenv.shape
    slots, share, _ = mask_ref.shape
    edges = in_ref.shape[0]
    per_chunk = edges // CHUNKS
    sec = lax.axis_index("sector")
    me = lax.axis_index("mpo")
    m_peers = [lax.rem(me + d, ranks) for d in range(1, ranks)]
    s_peers = [lax.rem(sec + d, sectors) for d in range(1, sectors)]

    lcopy = pltpu.make_async_copy(lenv_hbm, lenv, env_sem.at[0])
    rcopy = pltpu.make_async_copy(renv_hbm, renv, env_sem.at[1])
    rcopy.start()
    lcopy.start()

    barrier = pltpu.get_barrier_semaphore()
    for peer in m_peers:
        pl.semaphore_signal(barrier, inc=1, device_id=(sec, peer), device_id_type=MESH)
    for peer in s_peers:
        pl.semaphore_signal(barrier, inc=1, device_id=(peer, me), device_id_type=MESH)
    pl.semaphore_wait(barrier, ranks + sectors - 2)

    def to_rank(src, dst, send, recv, peer):
        return pltpu.make_async_remote_copy(
            src_ref=src, dst_ref=dst, send_sem=send, recv_sem=recv,
            device_id=(sec, peer), device_id_type=MESH,
        )

    def to_sector(src, dst, send, recv, peer):
        return pltpu.make_async_remote_copy(
            src_ref=src, dst_ref=dst, send_sem=send, recv_sem=recv,
            device_id=(peer, me), device_id_type=MESH,
        )

    def fold(value):
        return jnp.sum(value.reshape(slots * share, size), axis=0, keepdims=True)

    def add_up(index, rows):
        filler = [jnp.zeros((8 - len(rows), size), jnp.float32)] if len(rows) < 8 else []
        sum_m[index, me] = jnp.concatenate(rows + filler, axis=0)
        for peer in m_peers:
            to_rank(sum_m.at[index, me], sum_m.at[index, me],
                    sm_send.at[index, peer], sm_recv.at[index, me], peer).start()
        for peer in m_peers:
            to_rank(sum_m.at[index, peer], sum_m.at[index, peer],
                    sm_send.at[index, peer], sm_recv.at[index, peer], peer).wait()
        value = sum_m[index, 0]
        for i in range(1, ranks):
            value = value + sum_m[index, i]
        sum_s[index, sec] = value
        for peer in s_peers:
            to_sector(sum_s.at[index, sec], sum_s.at[index, sec],
                      ss_send.at[index, peer], ss_recv.at[index, sec], peer).start()
        for peer in s_peers:
            to_sector(sum_s.at[index, peer], sum_s.at[index, peer],
                      ss_send.at[index, peer], ss_recv.at[index, peer], peer).wait()
        value = sum_s[index, 0]
        for i in range(1, sectors):
            value = value + sum_s[index, i]
        return jnp.sum(value, axis=1, keepdims=True)

    first = pl.multiple_of(me * share, share)
    own_start = start_ref[:, pl.ds(first, share), :]
    norm = add_up(0, [fold(own_start * own_start)])[0:1, :]
    scale = 1.0 / jnp.sqrt(norm + 1e-06)
    basis[0] = own_start * scale[None]
    for j in range(1, APPLIES + 1):
        basis[j] = jnp.zeros((slots, share, size), jnp.float32)
    for m in range(ranks):
        gathered[0, m] = (
            start_ref[:, m * share:(m + 1) * share, :] * scale[None]
        ).astype(jnp.bfloat16)
    gram[...] = jnp.zeros_like(gram)
    for k in range(APPLIES):
        arrived[k, pl.ds(sec * capacity, capacity)] = jnp.zeros(
            (capacity, share, size), jnp.bfloat16)
    rcopy.wait()
    lcopy.wait()

    def apply(k, carry):
        @pl.when(k > 0)
        def _():
            for peer in m_peers:
                to_rank(gathered.at[k, peer], gathered.at[k, peer],
                        x_send.at[k, peer], x_recv.at[k, peer], peer).wait()

        def one_edge(e, carry):
            a, l, r = in_ref[e], left_ref[e], right_ref[e]
            x = jnp.concatenate([gathered[k, m, a] for m in range(ranks)], axis=0)
            acc = jnp.zeros((size, size), jnp.float32)
            for w in range(0, terms, GROUP):
                halves = []
                for v in range(w, w + GROUP, 2):
                    pair = jnp.concatenate([renv[v, r], renv[v + 1, r]], axis=1)
                    h = jnp.dot(x, pair, preferred_element_type=jnp.float32)
                    h = h.astype(jnp.bfloat16)
                    halves += [h[:, :size], h[:, size:]]
                half = jnp.concatenate(halves, axis=0)
                lefts = jnp.concatenate([lenv[v, l] for v in range(w, w + GROUP)], axis=1)
                acc = acc + jnp.dot(lefts, half, preferred_element_type=jnp.float32)
            out = acc.astype(jnp.bfloat16)
            for m in range(ranks):
                parts[k, m, e] = out[m * share:(m + 1) * share]
            return carry

        def part_copy(c, peer, slot):
            rows = pl.ds(c * per_chunk, per_chunk)
            return to_rank(parts.at[k, peer, rows], part_in.at[k, slot, rows],
                           p_send.at[k, c, peer], p_recv.at[k, c, slot], peer)

        def rank_range(c):
            done = [(c + 1) * per_chunk // (sectors - 1), c * per_chunk // (sectors - 1)]
            low, high = min(done[1], capacity), min(done[0], capacity)
            return (low, capacity) if c == CHUNKS - 1 else (low, high)

        def block_copy(c, peer, slot):
            low, high = rank_range(c)
            count = high - low
            return to_sector(packed.at[k, pl.ds(peer * capacity + low, count)],
                             arrived.at[k, pl.ds(slot * capacity + low, count)],
                             a_send.at[k, c, peer], a_recv.at[k, c, slot], peer)

        def finish(c):
            for peer in m_peers:
                part_copy(c, peer, peer).wait()
            rows = pl.ds(c * per_chunk, per_chunk)
            value = parts[k, me, rows].astype(jnp.float32)
            for peer in m_peers:
                value = value + part_in[k, peer, rows].astype(jnp.float32)
            total[k, rows] = value.astype(jnp.bfloat16)
            low, high = rank_range(c)
            if high > low:
                for peer in s_peers:
                    for i in range(low, high):
                        at = peer * capacity + i
                        packed[k, at] = total[k, source_ref[at]]
                    block_copy(c, peer, sec).start()

        for c in range(CHUNKS):
            lax.fori_loop(c * per_chunk, (c + 1) * per_chunk, one_edge, 0)
            for peer in m_peers:
                part_copy(c, peer, me).start()
            if c > 0:
                finish(c - 1)
        current = basis[k]
        gram_rows = [fold(current * basis[j]) for j in range(APPLIES)]
        finish(CHUNKS - 1)
        for c in range(CHUNKS):
            low, high = rank_range(c)
            if high > low:
                for peer in s_peers:
                    block_copy(c, peer, peer).wait()

        def take(t, acc):
            value = arrived[k, perm_ref[t]].astype(jnp.float32)
            acc = jnp.where(keep_ref[t] > 0, acc, 0.0) + value
            running[t] = acc
            return acc

        lax.fori_loop(0, (sectors - 1) * capacity, take, jnp.zeros((share, size), jnp.float32))
        for b in range(slots):
            block = running[last_ref[b]]
            images_ref[k, b] = jnp.where(has_ref[b] > 0, block, 0.0) * mask_ref[b]
        image = images_ref[k]
        current = basis[k]
        sums = add_up(1 + 2 * k, [fold(current * image)] + gram_rows)
        theta = sums[0:1, :]
        ritz_ref[k] = jnp.broadcast_to(theta, (8, size))
        gram[k] = jnp.broadcast_to(sums, (8, size))
        shift = theta[None]
        corr = mask_ref[...] * (image - shift * current) / jnp.maximum(
            jnp.abs(diag_ref[...] - shift), 1.0)
        sums = add_up(2 + 2 * k, [fold(corr * basis[j]) for j in range(APPLIES)]
                      + [fold(corr * corr)])
        proj = [sums[j:j + 1, :] for j in range(APPLIES)]
        length = sums[APPLIES:APPLIES + 1, :]
        ortho = corr
        for j in range(APPLIES):
            ortho = ortho - proj[j][None] * basis[j]
            length = length - 2.0 * proj[j] * proj[j]
        for i in range(APPLIES):
            for j in range(i + 1):
                inner = gram[i, 1 + j:2 + j, 0:1]
                times = 1.0 if i == j else 2.0
                length = length + times * proj[i] * proj[j] * inner
        new = ortho * (1.0 / jnp.sqrt(jnp.maximum(length, 0.0) + 1e-06))[None]
        basis[k + 1] = new

        @pl.when(k < APPLIES - 1)
        def _():
            gathered[k + 1, me] = new.astype(jnp.bfloat16)
            for peer in m_peers:
                to_rank(gathered.at[k + 1, me], gathered.at[k + 1, me],
                        x_send.at[k + 1, peer], x_recv.at[k + 1, me], peer).start()

        return carry

    lax.fori_loop(0, APPLIES, apply, 0)
    next_ref[...] = basis[APPLIES]


def per_device(
    guess,
    diag_shift,
    block_rows,
    block_cols,
    left_env,
    right_env,
    edge_input,
    edge_left,
    edge_right,
    edge_owner,
    edge_slot,
):
    slots, size, _ = guess.shape
    terms, envs, _, _ = left_env.shape
    sectors = lax.axis_size("sector")
    ranks = lax.axis_size("mpo")
    edges = edge_input.shape[0]
    capacity = max(2, 2 * edges // sectors)
    share = size // ranks
    first_row = lax.axis_index("mpo") * share
    places = sectors * capacity
    i32 = jnp.int32

    owner = edge_owner[:, 0]
    order = jnp.arange(edges, dtype=i32)
    earlier = (owner[:, None] == owner[None, :]) & (order[None, :] < order[:, None])
    rank = jnp.sum(earlier.astype(i32), axis=1)
    where_to = owner * capacity + rank
    hits = where_to[None, :] == jnp.arange(places, dtype=i32)[:, None]
    slot_ids = (jnp.sum(jnp.where(hits, edge_slot[None, :] + 1, 0), axis=1) - 1).reshape(
        sectors, capacity
    )
    key = rank * edges + order
    position = jnp.sum((key[None, :] < key[:, None]).astype(i32), axis=1)
    pick = position[None, :] == order[:, None]

    def sort_by(values):
        return jnp.sum(jnp.where(pick, values[None, :], 0), axis=1)

    source = jnp.sum(jnp.where(hits, position[None, :], 0), axis=1)

    ids = lax.all_to_all(slot_ids, "sector", split_axis=0, concat_axis=0, tiled=True).reshape(-1)
    place = jnp.arange(places, dtype=i32)
    ids = jnp.where(ids < 0, slots, ids)
    code = ids * places + place
    at = jnp.sum((code[None, :] < code[:, None]).astype(i32), axis=1)
    at_hits = at[None, :] == place[:, None]
    perm = jnp.sum(jnp.where(at_hits, place[None, :], 0), axis=1)
    sorted_ids = jnp.sum(jnp.where(at_hits, ids[None, :], 0), axis=1)
    keep = jnp.concatenate(
        [jnp.zeros((1,), i32), (sorted_ids[1:] == sorted_ids[:-1]).astype(i32)]
    )
    block = jnp.arange(slots, dtype=i32)
    upto = jnp.sum((ids[None, :] <= block[:, None]).astype(i32), axis=1)
    last = jnp.maximum(upto - 1, 0)
    has = jnp.max((ids[None, :] == block[:, None]).astype(i32), axis=1)

    rows_index = lax.broadcasted_iota(i32, guess.shape, 1)
    cols_index = lax.broadcasted_iota(i32, guess.shape, 2)
    mask = (
        (rows_index < block_rows[:, None, None]) & (cols_index < block_cols[:, None, None])
    ).astype(jnp.float32)
    start = mask * guess
    mask = lax.dynamic_slice_in_dim(mask, first_row, share, 1)
    diag = lax.dynamic_slice_in_dim(diag_shift, first_row, share, 1)

    f32, bf16 = jnp.float32, jnp.bfloat16
    sums = 1 + 2 * APPLIES
    dma = pltpu.SemaphoreType.DMA
    smem = pl.BlockSpec(memory_space=pltpu.SMEM)
    vmem = pl.BlockSpec(memory_space=pltpu.VMEM)
    hbm = pl.BlockSpec(memory_space=pl.ANY)
    images, final, ritz = pl.pallas_call(
        functools.partial(davidson_kernel, sectors, ranks, capacity),
        out_shape=(
            jax.ShapeDtypeStruct((APPLIES, slots, share, size), f32),
            jax.ShapeDtypeStruct((slots, share, size), f32),
            jax.ShapeDtypeStruct((APPLIES, 8, size), f32),
        ),
        in_specs=[smem] * 8 + [vmem] * 3 + [hbm] * 2,
        out_specs=(vmem, vmem, vmem),
        scratch_shapes=[
            pltpu.VMEM((terms, envs, size, size), bf16),
            pltpu.VMEM((terms, envs, size, size), bf16),
            pltpu.VMEM((APPLIES + 1, slots, share, size), f32),
            pltpu.VMEM((APPLIES, ranks, slots, share, size), bf16),
            pltpu.VMEM((APPLIES, ranks, edges, share, size), bf16),
            pltpu.VMEM((APPLIES, ranks, edges, share, size), bf16),
            pltpu.VMEM((APPLIES, edges, share, size), bf16),
            pltpu.VMEM((APPLIES, places, share, size), bf16),
            pltpu.VMEM((APPLIES, places, share, size), bf16),
            pltpu.VMEM((places, share, size), f32),
            pltpu.VMEM((APPLIES, 8, size), f32),
            pltpu.VMEM((sums, ranks, 8, size), f32),
            pltpu.VMEM((sums, sectors, 8, size), f32),
            dma((2,)),
            dma((APPLIES, ranks)),
            dma((APPLIES, ranks)),
            dma((APPLIES, CHUNKS, ranks)),
            dma((APPLIES, CHUNKS, ranks)),
            dma((APPLIES, CHUNKS, sectors)),
            dma((APPLIES, CHUNKS, sectors)),
            dma((sums, ranks)),
            dma((sums, ranks)),
            dma((sums, sectors)),
            dma((sums, sectors)),
        ],
        compiler_params=pltpu.CompilerParams(
            collective_id=0, has_side_effects=True, vmem_limit_bytes=56 * 1024 * 1024
        ),
        cost_estimate=pl.CostEstimate(
            flops=APPLIES * edges * terms * 4 * size**3,
            bytes_accessed=2 * terms * envs * size * size * 2,
            transcendentals=0,
        ),
        name="davidson",
    )(
        sort_by(edge_input),
        sort_by(edge_left),
        sort_by(edge_right),
        source,
        perm,
        keep,
        last,
        has,
        start,
        mask,
        diag,
        left_env,
        right_env,
    )
    return (images, final, ritz[:, 0, 0])


def solution(mesh):
    return jax.shard_map(
        per_device,
        mesh=mesh,
        in_specs=(
            P("sector", None, None),
            P("sector", None, None),
            P("sector"),
            P("sector"),
            P("mpo", "sector", None, None),
            P("mpo", "sector", None, None),
            P("sector"),
            P("sector"),
            P("sector"),
            P("sector", None),
            P("sector"),
        ),
        out_specs=(P(None, "sector", "mpo", None), P("sector", "mpo", None), P()),
        check_vma=False,
    )
```

time: 890 us -> 217 us (0.24)
  waiting for transfers between devices: 261 us -> 0.01 us
  matrix products: 253 us -> 0 us
  Pallas kernels: 0 us -> 190 us
  blocking collectives: 138 us -> 0 us
  local copies, waits for them, and re-layouts: 144 us -> 7.14 us
  other arithmetic: 41.1 us -> 11.9 us
  between operations: 24.8 us -> 0.68 us
  starting transfers between devices: 22.7 us -> 7.28 us
    dot_general x54 -> x0, matrix products: 253 us -> none  [the longest x48 233 us: one_term(): jnp.einsum('eij,ejk->eik', left_term[edge_left], half, preferred_element_...]
    pallas_call x0 -> x1, Pallas kernels: none -> 190 us  [per_device(): pl.pallas_call(functools.partial(davidson_kernel, sectors, ranks, capacit...]
    all_to_all x4 -> x1, waiting for transfers between devices: 145 us -> 0.01 us  [per_device(): lax.all_to_all(slot_ids, 'sector', split_axis=0, concat_axis=0, tiled=True)]
    psum x7 -> x0, blocking collectives: 138 us -> none  [add_up(): return lax.psum(values, 'sector')]
    gather x99 -> x0, local copies, waits for them, and re-layouts: 76.9 us -> none  [the longest x48 35.9 us: one_term(): left_term[edge_left]]
    reduce_scatter x3 -> x0, waiting for transfers between devices: 67.8 us -> none  [apply_hamiltonian(): lax.psum_scatter(rounded_terms.astype(jnp.bfloat16), 'mpo', scatter_dimen...]
    squeeze x48 -> x0, local copies, waits for them, and re-layouts: 60.9 us -> none  [apply_hamiltonian(): lax.scan(one_term, jnp.zeros((edges, size, size), jnp.float32), (left_env...]
    all_gather x3 -> x0, waiting for transfers between devices: 48.3 us -> none  [deliver(): whole = lax.all_gather(rounded, 'mpo', axis=1, tiled=True)]
  transfers between devices with their start and end apart: 10 -> 1, of which waited for: 9 -> 0; matrix products, arithmetic and copies ran while one was open for 1% -> 3% of each run, Pallas kernels for 0% -> 0%
where the time goes in v1:
time: 217 us
  Pallas kernels  190 us (88%)
  other arithmetic  11.9 us (5%)
  starting transfers between devices  7.28 us (3%)
  local copies, waits for them, and re-layouts  7.14 us (3%)
    pallas_call x1, Pallas kernels, per_device(): pl.pallas_call(functools.partial(davidson_kernel, sectors, ranks, capacit...  190 us
    all_to_all x1, starting transfers between devices, per_device(): lax.all_to_all(slot_ids, 'sector', split_axis=0, concat_axis=0, tiled=True)  7.28 us
  transfers between devices with their start and end apart: 1, of which 0 were waited for; matrix products, arithmetic and copies ran while one was open for 3% of the time, Pallas kernels for 0%

profile of v1, /device:TPU:0, one launch (start us, length us, event | category | flops | bytes accessed | tf_op | source)
XLA Modules:
  0.0 217.0 jit_solution(17130312134078907311)
XLA Ops:
  0.6 0.9 convert_reduce_fusion.2
  1.6 0.7 multiply_add_fusion
  2.3 0.2 convert_reduce_fusion.1
  2.4 0.6 select_reduce_fusion.2
  3.1 0.7 sub.10
  3.8 7.3 %all-to-all-start = ((s32[8,1,8]{2,1,0:T(1,128)}), s32[8,1,8]{2,1,0:T(1,128)S(1)}, u32[]{:S(2)}, u32[]{:S(2)}) async-start(s32[8,1,8]{2,1,0:T(1,128)} %bitcast.1), calls=%async_computation | async-start | bytes 8192 | tf_op jit(solution)/shard_map/all_to_all | solution.py:303
  11.1 0.7 constant_dynamic-slice_fusion.diag_ref
  11.8 1.1 fusion
  12.9 0.7 dynamic-slice_convert_fusion.mask_ref
  13.6 2.9 %broadcast_select_fusion.start_ref = f32[16,128,128]{2,1,0:T(8,128)} fusion(f32[16,128,128]{2,1,0:T(8,128)} %param.11, s32[16]{0:T(128)} %param.14, s32[16]{0:T(128)} %param.13), kind=kLoop, calls=%fused_computation.3 | loop fusion | flops 1048576 | bytes 2097280 | tf_op jit(solution)/shard_map/mul | solution.py:324
  16.5 1.3 select_reduce_fusion.4
  17.8 0.6 broadcast.86
  18.4 0.7 reduce.5
  19.1 0.1 reshape.93
  19.2 0.2 convert_reduce_fusion
  19.4 0.6 convert_reduce_fusion.3
  20.0 0.7 select_reduce_fusion
  20.7 0.1 slice_compare_fusion
  20.8 0.6 add_maximum_fusion.last_ref
  21.4 0.6 add_convert_fusion.keep_ref
  22.0 190.0 %davidson.1 = (f32[3,16,32,128]{3,2,1,0:T(8,128)}, f32[16,32,128]{2,1,0:T(8,128)}, f32[3,8,128]{2,1,0:T(8,128)}) custom-call(s32[32]{0:T(128)} %get-tuple-element.17.in_ref, s32[32]{0:T(128)} %get-tuple-element.16.left_ref, s32[32]{0:T(128)} %get-tuple-element.15.right_ref, s32[64]{0:T(128)} %get-tuple-element.14.source_ref, s32[64]{0:T(128)} %get-tuple-element.12.perm_ref, ...), custom_call_target="tpu_custom_call" | custom-call | flops 12884901888 | bytes 16777216 | tf_op jit(solution)/shard_map/davidson/pallas_call | solution.py:334
  211.9 1.3 slice_reduce_fusion
  213.3 2.1 copy.18
  215.3 1.7 copy.19
  (5 shorter events, 0.0 us)
Async XLA Ops:
  0.6 10.4 %copy-start = (f32[16,128,128]{2,1,0:T(8,128)S(1)}, f32[16,128,128]{2,1,0:T(8,128)}, u32[]{:S(2)}) copy-start(f32[16,128,128]{2,1,0:T(8,128)} %param.12) | copy-start | bytes 3145732
  3.8 14.1 %all-to-all-start = ((s32[8,1,8]{2,1,0:T(1,128)}), s32[8,1,8]{2,1,0:T(1,128)S(1)}, u32[]{:S(2)}, u32[]{:S(2)}) async-start(s32[8,1,8]{2,1,0:T(1,128)} %bitcast.1), calls=%async_computation | async-start | bytes 8192 | tf_op jit(solution)/shard_map/all_to_all | solution.py:303

commit v2 on v1

--- a/solution.py
+++ b/solution.py
@@ -8,7 +8,8 @@
 from jax.sharding import PartitionSpec as P
 
 APPLIES = 3
-CHUNKS = 4
+CHUNKS = 8
+ABREAST = 2
 GROUP = 4
 MESH = pl.DeviceIdType.MESH
 
@@ -21,12 +22,10 @@
     left_ref,
     right_ref,
     source_ref,
-    perm_ref,
-    keep_ref,
-    last_ref,
-    has_ref,
-    start_ref,
-    mask_ref,
+    rows_ref,
+    cols_ref,
+    ids_ref,
+    guess_ref,
     diag_ref,
     lenv_hbm,
     renv_hbm,
@@ -42,7 +41,8 @@
     total,
     packed,
     arrived,
-    running,
+    ids,
+    mask_ref,
     gram,
     sum_m,
     sum_s,
@@ -57,6 +57,8 @@
     sm_recv,
     ss_send,
     ss_recv,
+    id_send,
+    id_recv,
 ):
     terms, _, size, _ = lenv.shape
     slots, share, _ = mask_ref.shape
@@ -118,21 +120,38 @@
             value = value + sum_s[index, i]
         return jnp.sum(value, axis=1, keepdims=True)
 
+    def id_copy(peer, slot):
+        return to_sector(ids_ref.at[pl.ds(peer * capacity, capacity)],
+                         ids.at[pl.ds(slot * capacity, capacity)],
+                         id_send.at[peer], id_recv.at[slot], peer)
+
+    for peer in s_peers:
+        id_copy(peer, sec).start()
+    ids[pl.ds(sec * capacity, capacity)] = jnp.full((capacity, 8, size), -1, jnp.int32)
+
     first = pl.multiple_of(me * share, share)
-    own_start = start_ref[:, pl.ds(first, share), :]
+    row = lax.broadcasted_iota(jnp.int32, (share, size), 0)
+    col = lax.broadcasted_iota(jnp.int32, (share, size), 1)
+    for b in range(slots):
+        inside = (row + first < rows_ref[b]) & (col < cols_ref[b])
+        mask_ref[b] = jnp.where(inside, 1.0, 0.0)
+    own_start = guess_ref[:, pl.ds(first, share), :] * mask_ref[...]
     norm = add_up(0, [fold(own_start * own_start)])[0:1, :]
     scale = 1.0 / jnp.sqrt(norm + 1e-06)
     basis[0] = own_start * scale[None]
     for j in range(1, APPLIES + 1):
         basis[j] = jnp.zeros((slots, share, size), jnp.float32)
-    for m in range(ranks):
-        gathered[0, m] = (
-            start_ref[:, m * share:(m + 1) * share, :] * scale[None]
-        ).astype(jnp.bfloat16)
+    for b in range(slots):
+        for m in range(ranks):
+            inside = (row + m * share < rows_ref[b]) & (col < cols_ref[b])
+            part = guess_ref[b, m * share:(m + 1) * share, :]
+            gathered[0, m, b] = (jnp.where(inside, part, 0.0) * scale).astype(jnp.bfloat16)
     gram[...] = jnp.zeros_like(gram)
     for k in range(APPLIES):
         arrived[k, pl.ds(sec * capacity, capacity)] = jnp.zeros(
             (capacity, share, size), jnp.bfloat16)
+    for peer in s_peers:
+        id_copy(peer, peer).wait()
     rcopy.wait()
     lcopy.wait()
 
@@ -143,24 +162,32 @@
                 to_rank(gathered.at[k, peer], gathered.at[k, peer],
                         x_send.at[k, peer], x_recv.at[k, peer], peer).wait()
 
-        def one_edge(e, carry):
-            a, l, r = in_ref[e], left_ref[e], right_ref[e]
-            x = jnp.concatenate([gathered[k, m, a] for m in range(ranks)], axis=0)
-            acc = jnp.zeros((size, size), jnp.float32)
+        def some_edges(edge_list):
+            xs, lefts, rights = [], [], []
+            for e in edge_list:
+                a = in_ref[e]
+                lefts.append(left_ref[e])
+                rights.append(right_ref[e])
+                xs.append(jnp.concatenate([gathered[k, m, a] for m in range(ranks)], axis=0))
+            accs = [jnp.zeros((size, size), jnp.float32) for _ in edge_list]
             for w in range(0, terms, GROUP):
                 halves = []
-                for v in range(w, w + GROUP, 2):
-                    pair = jnp.concatenate([renv[v, r], renv[v + 1, r]], axis=1)
-                    h = jnp.dot(x, pair, preferred_element_type=jnp.float32)
-                    h = h.astype(jnp.bfloat16)
-                    halves += [h[:, :size], h[:, size:]]
-                half = jnp.concatenate(halves, axis=0)
-                lefts = jnp.concatenate([lenv[v, l] for v in range(w, w + GROUP)], axis=1)
-                acc = acc + jnp.dot(lefts, half, preferred_element_type=jnp.float32)
-            out = acc.astype(jnp.bfloat16)
-            for m in range(ranks):
-                parts[k, m, e] = out[m * share:(m + 1) * share]
-            return carry
+                for x, r in zip(xs, rights):
+                    half = []
+                    for v in range(w, w + GROUP, 2):
+                        pair = jnp.concatenate([renv[v, r], renv[v + 1, r]], axis=1)
+                        h = jnp.dot(x, pair, preferred_element_type=jnp.float32)
+                        h = h.astype(jnp.bfloat16)
+                        half += [h[:, :size], h[:, size:]]
+                    halves.append(jnp.concatenate(half, axis=0))
+                for i, l in enumerate(lefts):
+                    wide = jnp.concatenate([lenv[v, l] for v in range(w, w + GROUP)], axis=1)
+                    accs[i] = accs[i] + jnp.dot(
+                        wide, halves[i], preferred_element_type=jnp.float32)
+            for e, acc in zip(edge_list, accs):
+                out = acc.astype(jnp.bfloat16)
+                for m in range(ranks):
+                    parts[k, m, e] = out[m * share:(m + 1) * share]
 
         def part_copy(c, peer, slot):
             rows = pl.ds(c * per_chunk, per_chunk)
@@ -168,8 +195,8 @@
                            p_send.at[k, c, peer], p_recv.at[k, c, slot], peer)
 
         def rank_range(c):
-            done = [(c + 1) * per_chunk // (sectors - 1), c * per_chunk // (sectors - 1)]
-            low, high = min(done[1], capacity), min(done[0], capacity)
+            low = min(c * per_chunk // (sectors - 1), capacity)
+            high = min((c + 1) * per_chunk // (sectors - 1), capacity)
             return (low, capacity) if c == CHUNKS - 1 else (low, high)
 
         def block_copy(c, peer, slot):
@@ -179,7 +206,7 @@
                              arrived.at[k, pl.ds(slot * capacity + low, count)],
                              a_send.at[k, c, peer], a_recv.at[k, c, slot], peer)
 
-        def finish(c):
+        def add_parts(c):
             for peer in m_peers:
                 part_copy(c, peer, peer).wait()
             rows = pl.ds(c * per_chunk, per_chunk)
@@ -187,39 +214,57 @@
             for peer in m_peers:
                 value = value + part_in[k, peer, rows].astype(jnp.float32)
             total[k, rows] = value.astype(jnp.bfloat16)
+
+        def send_blocks(c):
             low, high = rank_range(c)
-            if high > low:
-                for peer in s_peers:
-                    for i in range(low, high):
-                        at = peer * capacity + i
-                        packed[k, at] = total[k, source_ref[at]]
-                    block_copy(c, peer, sec).start()
-
-        for c in range(CHUNKS):
-            lax.fori_loop(c * per_chunk, (c + 1) * per_chunk, one_edge, 0)
+            for peer in s_peers:
+                for i in range(low, high):
+                    at = peer * capacity + i
+                    packed[k, at] = total[k, source_ref[at]]
+                block_copy(c, peer, sec).start()
+
+        sending = [c for c in range(CHUNKS) if rank_range(c)[1] > rank_range(c)[0]]
+
+        def chunk(c, carry):
+            for i in range(0, per_chunk, ABREAST):
+                some_edges([c * per_chunk + i + j for j in range(ABREAST)])
             for peer in m_peers:
                 part_copy(c, peer, me).start()
-            if c > 0:
-                finish(c - 1)
+
+            @pl.when(c > 0)
+            def _():
+                add_parts(c - 1)
+
+            for s in sending:
+                if s < CHUNKS - 1:
+                    pl.when(c == s + 1)(functools.partial(send_blocks, s))
+            return carry
+
+        lax.fori_loop(0, CHUNKS, chunk, 0)
         current = basis[k]
         gram_rows = [fold(current * basis[j]) for j in range(APPLIES)]
-        finish(CHUNKS - 1)
-        for c in range(CHUNKS):
-            low, high = rank_range(c)
-            if high > low:
-                for peer in s_peers:
-                    block_copy(c, peer, peer).wait()
-
-        def take(t, acc):
-            value = arrived[k, perm_ref[t]].astype(jnp.float32)
-            acc = jnp.where(keep_ref[t] > 0, acc, 0.0) + value
-            running[t] = acc
-            return acc
-
-        lax.fori_loop(0, (sectors - 1) * capacity, take, jnp.zeros((share, size), jnp.float32))
-        for b in range(slots):
-            block = running[last_ref[b]]
-            images_ref[k, b] = jnp.where(has_ref[b] > 0, block, 0.0) * mask_ref[b]
+        add_parts(CHUNKS - 1)
+        if CHUNKS - 1 in sending:
+            send_blocks(CHUNKS - 1)
+        for c in sending:
+            for peer in s_peers:
+                block_copy(c, peer, peer).wait()
+
+        for low in range(0, slots, 8):
+            count = min(8, slots - low)
+
+            def take(t, accs):
+                value = arrived[k, t].astype(jnp.float32).reshape(share // 8, 8, size)
+                tag = ids[t]
+                return tuple(
+                    acc + jnp.where((tag == low + b)[None], value, 0.0)
+                    for b, acc in enumerate(accs)
+                )
+
+            zero = jnp.zeros((share // 8, 8, size), jnp.float32)
+            accs = lax.fori_loop(0, sectors * capacity, take, (zero,) * count, unroll=2)
+            for b in range(count):
+                images_ref[k, low + b] = accs[b].reshape(share, size) * mask_ref[low + b]
         image = images_ref[k]
         current = basis[k]
         sums = add_up(1 + 2 * k, [fold(current * image)] + gram_rows)
@@ -228,7 +273,7 @@
         gram[k] = jnp.broadcast_to(sums, (8, size))
         shift = theta[None]
         corr = mask_ref[...] * (image - shift * current) / jnp.maximum(
-            jnp.abs(diag_ref[...] - shift), 1.0)
+            jnp.abs(diag_ref[:, pl.ds(first, share), :] - shift), 1.0)
         sums = add_up(2 + 2 * k, [fold(corr * basis[j]) for j in range(APPLIES)]
                       + [fold(corr * corr)])
         proj = [sums[j:j + 1, :] for j in range(APPLIES)]
@@ -278,7 +323,6 @@
     edges = edge_input.shape[0]
     capacity = max(2, 2 * edges // sectors)
     share = size // ranks
-    first_row = lax.axis_index("mpo") * share
     places = sectors * capacity
     i32 = jnp.int32
 
@@ -288,42 +332,15 @@
     rank = jnp.sum(earlier.astype(i32), axis=1)
     where_to = owner * capacity + rank
     hits = where_to[None, :] == jnp.arange(places, dtype=i32)[:, None]
-    slot_ids = (jnp.sum(jnp.where(hits, edge_slot[None, :] + 1, 0), axis=1) - 1).reshape(
-        sectors, capacity
-    )
+    slot_ids = jnp.sum(jnp.where(hits, edge_slot[None, :] + 1, 0), axis=1) - 1
     key = rank * edges + order
     position = jnp.sum((key[None, :] < key[:, None]).astype(i32), axis=1)
     pick = position[None, :] == order[:, None]
 
-    def sort_by(values):
-        return jnp.sum(jnp.where(pick, values[None, :], 0), axis=1)
-
+    tables = jnp.stack([edge_input, edge_left, edge_right])
+    tables = jnp.sum(jnp.where(pick[None], tables[:, None, :], 0), axis=2)
     source = jnp.sum(jnp.where(hits, position[None, :], 0), axis=1)
-
-    ids = lax.all_to_all(slot_ids, "sector", split_axis=0, concat_axis=0, tiled=True).reshape(-1)
-    place = jnp.arange(places, dtype=i32)
-    ids = jnp.where(ids < 0, slots, ids)
-    code = ids * places + place
-    at = jnp.sum((code[None, :] < code[:, None]).astype(i32), axis=1)
-    at_hits = at[None, :] == place[:, None]
-    perm = jnp.sum(jnp.where(at_hits, place[None, :], 0), axis=1)
-    sorted_ids = jnp.sum(jnp.where(at_hits, ids[None, :], 0), axis=1)
-    keep = jnp.concatenate(
-        [jnp.zeros((1,), i32), (sorted_ids[1:] == sorted_ids[:-1]).astype(i32)]
-    )
-    block = jnp.arange(slots, dtype=i32)
-    upto = jnp.sum((ids[None, :] <= block[:, None]).astype(i32), axis=1)
-    last = jnp.maximum(upto - 1, 0)
-    has = jnp.max((ids[None, :] == block[:, None]).astype(i32), axis=1)
-
-    rows_index = lax.broadcasted_iota(i32, guess.shape, 1)
-    cols_index = lax.broadcasted_iota(i32, guess.shape, 2)
-    mask = (
-        (rows_index < block_rows[:, None, None]) & (cols_index < block_cols[:, None, None])
-    ).astype(jnp.float32)
-    start = mask * guess
-    mask = lax.dynamic_slice_in_dim(mask, first_row, share, 1)
-    diag = lax.dynamic_slice_in_dim(diag_shift, first_row, share, 1)
+    ids = jnp.broadcast_to(slot_ids[:, None, None], (places, 8, size))
 
     f32, bf16 = jnp.float32, jnp.bfloat16
     sums = 1 + 2 * APPLIES
@@ -338,7 +355,7 @@
             jax.ShapeDtypeStruct((slots, share, size), f32),
             jax.ShapeDtypeStruct((APPLIES, 8, size), f32),
         ),
-        in_specs=[smem] * 8 + [vmem] * 3 + [hbm] * 2,
+        in_specs=[smem] * 6 + [vmem] * 3 + [hbm] * 2,
         out_specs=(vmem, vmem, vmem),
         scratch_shapes=[
             pltpu.VMEM((terms, envs, size, size), bf16),
@@ -350,7 +367,8 @@
             pltpu.VMEM((APPLIES, edges, share, size), bf16),
             pltpu.VMEM((APPLIES, places, share, size), bf16),
             pltpu.VMEM((APPLIES, places, share, size), bf16),
-            pltpu.VMEM((places, share, size), f32),
+            pltpu.VMEM((places, 8, size), i32),
+            pltpu.VMEM((slots, share, size), f32),
             pltpu.VMEM((APPLIES, 8, size), f32),
             pltpu.VMEM((sums, ranks, 8, size), f32),
             pltpu.VMEM((sums, sectors, 8, size), f32),
@@ -365,6 +383,8 @@
             dma((sums, ranks)),
             dma((sums, sectors)),
             dma((sums, sectors)),
+            dma((sectors,)),
+            dma((sectors,)),
         ],
         compiler_params=pltpu.CompilerParams(
             collective_id=0, has_side_effects=True, vmem_limit_bytes=56 * 1024 * 1024
@@ -376,17 +396,15 @@
         ),
         name="davidson",
     )(
-        sort_by(edge_input),
-        sort_by(edge_left),
-        sort_by(edge_right),
+        tables[0],
+        tables[1],
+        tables[2],
         source,
-        perm,
-        keep,
-        last,
-        has,
-        start,
-        mask,
-        diag,
+        block_rows,
+        block_cols,
+        ids,
+        guess,
+        diag_shift,
         left_env,
         right_env,
     )

time: 217 us -> 184 us (0.85)
  Pallas kernels: 190 us -> 174 us
  other arithmetic: 11.9 us -> 3.27 us
  starting transfers between devices: 7.28 us -> 0 us
    pallas_call x1, Pallas kernels: 190 us -> 174 us  [per_device(): pl.pallas_call(functools.partial(davidson_kernel, sectors, ranks, capacit...]
    all_to_all x1 -> x0, starting transfers between devices: 7.28 us -> none  [per_device(): lax.all_to_all(slot_ids, 'sector', split_axis=0, concat_axis=0, tiled=True)]
    mul x1 -> x0, other arithmetic: 2.88 us -> none  [per_device(): start = mask * guess]
  transfers between devices with their start and end apart: 1 -> 0, of which waited for: 0 -> 0; matrix products, arithmetic and copies ran while one was open for 3% -> 0% of each run, Pallas kernels for 0% -> 0%
where the time goes in v2:
time: 184 us
  Pallas kernels  174 us (95%)
  local copies, waits for them, and re-layouts  6.42 us (3%)
  other arithmetic  3.27 us (2%)
    pallas_call x1, Pallas kernels, per_device(): pl.pallas_call(functools.partial(davidson_kernel, sectors, ranks, capacit...  174 us
    unnamed x2, local copies, waits for them, and re-layouts  3.73 us

profile of v2, /device:TPU:0, one launch (start us, length us, event | category | flops | bytes accessed | tf_op | source)
XLA Modules:
  0.0 183.9 jit_solution(14456565497090054381)
XLA Ops:
  0.6 0.9 convert_reduce_fusion.1
  1.5 0.7 multiply_add_fusion
  2.2 0.2 convert_reduce_fusion
  2.4 0.6 select_reduce_fusion.1
  3.0 0.7 pad_add_fusion
  3.8 0.1 select_reduce_fusion
  3.9 0.5 slice_bitcast_fusion
  4.4 0.8 broadcast_in_dim.62.ids_ref
  5.3 173.5 %davidson.1 = (f32[3,16,32,128]{3,2,1,0:T(8,128)}, f32[16,32,128]{2,1,0:T(8,128)}, f32[3,8,128]{2,1,0:T(8,128)}) custom-call(s32[32]{0:T(128)} %get-tuple-element.13.in_ref, s32[32]{0:T(128)} %get-tuple-element.12.left_ref, s32[32]{0:T(128)} %get-tuple-element.11.right_ref, s32[64]{0:T(128)} %get-tuple-element.10.source_ref, s32[16]{0:T(128)} %rows_ref.1, ...), custom_call_target="tpu_custom_call" | custom-call | flops 12884901888 | bytes 16777216 | tf_op jit(solution)/shard_map/davidson/pallas_call | solution.py:351
  178.8 1.3 slice_reduce_fusion
  180.1 2.1 %copy.16 = f32[3,16,32,128]{3,2,1,0:T(8,128)} copy(f32[3,16,32,128]{3,2,1,0:T(8,128)} %get-tuple-element.20) | data formatting | bytes 1572864
  182.2 1.7 copy.17
  (2 shorter events, 0.0 us)

commit v3 on v2

--- a/solution.py
+++ b/solution.py
@@ -9,7 +9,7 @@
 
 APPLIES = 3
 CHUNKS = 8
-ABREAST = 2
+ABREAST = 4
 GROUP = 4
 MESH = pl.DeviceIdType.MESH
 
@@ -49,6 +49,7 @@
     env_sem,
     x_send,
     x_recv,
+    x_pass,
     p_send,
     p_recv,
     a_send,
@@ -92,6 +93,14 @@
             src_ref=src, dst_ref=dst, send_sem=send, recv_sem=recv,
             device_id=(peer, me), device_id_type=MESH,
         )
+
+    partner = me + 1 - 2 * lax.rem(me, 2)
+    alike = [lax.rem(me + d, ranks) for d in range(2, ranks, 2)]
+    alike_across = [lax.rem(partner + d, ranks) for d in range(2, ranks, 2)]
+
+    def x_copy(k, origin, peer, send):
+        return to_rank(gathered.at[k, origin], gathered.at[k, origin],
+                       send, x_recv.at[k, origin], peer)
 
     def fold(value):
         return jnp.sum(value.reshape(slots * share, size), axis=0, keepdims=True)
@@ -158,9 +167,13 @@
     def apply(k, carry):
         @pl.when(k > 0)
         def _():
-            for peer in m_peers:
-                to_rank(gathered.at[k, peer], gathered.at[k, peer],
-                        x_send.at[k, peer], x_recv.at[k, peer], peer).wait()
+            for peer in alike:
+                x_copy(k, peer, peer, x_send.at[k, peer]).wait()
+                x_copy(k, peer, partner, x_pass.at[k, peer]).start()
+            x_copy(k, partner, partner, x_send.at[k, partner]).wait()
+            for peer, across in zip(alike, alike_across):
+                x_copy(k, peer, partner, x_pass.at[k, peer]).wait_send()
+                x_copy(k, across, partner, x_pass.at[k, peer]).wait_recv()
 
         def some_edges(edge_list):
             xs, lefts, rights = [], [], []
@@ -293,9 +306,8 @@
         @pl.when(k < APPLIES - 1)
         def _():
             gathered[k + 1, me] = new.astype(jnp.bfloat16)
-            for peer in m_peers:
-                to_rank(gathered.at[k + 1, me], gathered.at[k + 1, me],
-                        x_send.at[k + 1, peer], x_recv.at[k + 1, me], peer).start()
+            for peer in alike + [partner]:
+                x_copy(k + 1, me, peer, x_send.at[k + 1, peer]).start()
 
         return carry
 
@@ -373,6 +385,7 @@
             pltpu.VMEM((sums, ranks, 8, size), f32),
             pltpu.VMEM((sums, sectors, 8, size), f32),
             dma((2,)),
+            dma((APPLIES, ranks)),
             dma((APPLIES, ranks)),
             dma((APPLIES, ranks)),
             dma((APPLIES, CHUNKS, ranks)),

time: 184 us -> 176 us (0.957)
  Pallas kernels: 174 us -> 165 us
    pallas_call x1, Pallas kernels: 174 us -> 165 us  [per_device(): pl.pallas_call(functools.partial(davidson_kernel, sectors, ranks, capacit...]
where the time goes in v3:
time: 176 us
  Pallas kernels  165 us (94%)
  local copies, waits for them, and re-layouts  6.42 us (4%)
  other arithmetic  3.27 us (2%)
    pallas_call x1, Pallas kernels, per_device(): pl.pallas_call(functools.partial(davidson_kernel, sectors, ranks, capacit...  165 us
    unnamed x2, local copies, waits for them, and re-layouts  3.73 us

profile of v3, /device:TPU:0, one launch (start us, length us, event | category | flops | bytes accessed | tf_op | source)
XLA Modules:
  0.0 175.8 jit_solution(12933972740553220597)
XLA Ops:
  0.6 0.9 convert_reduce_fusion.1
  1.5 0.7 multiply_add_fusion
  2.2 0.2 convert_reduce_fusion
  2.4 0.6 select_reduce_fusion.1
  3.0 0.7 pad_add_fusion
  3.8 0.1 select_reduce_fusion
  3.9 0.5 slice_bitcast_fusion
  4.4 0.8 broadcast_in_dim.62.ids_ref
  5.3 165.4 %davidson.1 = (f32[3,16,32,128]{3,2,1,0:T(8,128)}, f32[16,32,128]{2,1,0:T(8,128)}, f32[3,8,128]{2,1,0:T(8,128)}) custom-call(s32[32]{0:T(128)} %get-tuple-element.13.in_ref, s32[32]{0:T(128)} %get-tuple-element.12.left_ref, s32[32]{0:T(128)} %get-tuple-element.11.right_ref, s32[64]{0:T(128)} %get-tuple-element.10.source_ref, s32[16]{0:T(128)} %rows_ref.1, ...), custom_call_target="tpu_custom_call" | custom-call | flops 12884901888 | bytes 16777216 | tf_op jit(solution)/shard_map/davidson/pallas_call | solution.py:363
  170.7 1.3 slice_reduce_fusion
  172.0 2.1 %copy.16 = f32[3,16,32,128]{3,2,1,0:T(8,128)} copy(f32[3,16,32,128]{3,2,1,0:T(8,128)} %get-tuple-element.20) | data formatting | bytes 1572864
  174.1 1.7 copy.17
  (2 shorter events, 0.0 us)
